TPU v7x, 32 devices: a whole 2x2x4 slice. The times are simulated.
32 devices in a mesh: grp: 2 (over x), doc: 16 (over z, y, core).
Axes of the slice: x: 2, y: 2, z: 4, core: 2. Of those that a mesh axis runs over, the one named last changes fastest.
Arguments:
- queries: bfloat16 [128, 2, 4096], P('doc'), may hold values from -6 to 6
- documents: bfloat16 [16384, 2, 4096], P(('grp', 'doc')), parts along dimension 0, may hold values from -450 to 450
- eigvals: float32 [2, 64, 64], replicated, may hold values from 0.01 to 1
- basis_in: float32 [2, 64, 64], replicated, may hold values from -1 to 1, as said below
- basis_out: float32 [2, 64, 64], replicated, may hold values from -1 to 1, as said below
Outputs:
- standardized: float32 [16384, 128], P(('grp', 'doc')), parts along dimension 0
There are 2 independent parts, one for each index of `grp`. A program takes and returns all parts, laid end to end along the dimension named above; an argument that names none is the same for every part. Nothing has to cross between parts.
Inputs may be any that keep to these rules, and one draw needn't show every extreme that they name: `basis_in`: each layer's matrix is orthogonal. `basis_out`: each layer's matrix is orthogonal.
All inputs are finite; a program needn't handle non-finite values.
Results may differ from a plain program's by a relative error of at most 0.003.
Values may be sent and summed in bfloat16 or wider, within the bound.
A program may use at most 128 MiB of HBM per device.

v0:
```python
import jax
import jax.numpy as jnp
from jax import lax
from jax.sharding import PartitionSpec as P

DOUT = 64
DIN = 64


damp_scale = 0.1
eps_var = 1e-06


def precondition(grads, eigvals, basis_in, basis_out):
    count = grads.shape[0]
    layer_count = grads.shape[1]
    square = grads.astype(jnp.float32).reshape(count, layer_count, DOUT, DIN)
    damping = damp_scale * jnp.mean(eigvals, axis=(1, 2), keepdims=True)
    rotated = jnp.einsum(
        "lai,qlab,lbj->qlij", basis_out, square, basis_in, precision=lax.Precision.HIGHEST
    )
    scaled = rotated / (eigvals + damping)[None]
    back = jnp.einsum(
        "lia,qlab,ljb->qlij", basis_out, scaled, basis_in, precision=lax.Precision.HIGHEST
    )
    return back.reshape(count, layer_count, DOUT * DIN).astype(jnp.bfloat16)


def layer_scores(doc_layer, query_layer):
    return jnp.einsum(
        "dp,qp->dq",
        doc_layer,
        lax.all_gather(query_layer, "doc", axis=0, tiled=True),
        preferred_element_type=jnp.float32,
    )


def shards(queries, documents, eigvals, basis_in, basis_out):
    doc_rows = documents.shape[0]
    outgoing = precondition(queries, eigvals, basis_in, basis_out)
    scores = layer_scores(documents[:, 0, :], outgoing[:, 0, :])
    scores = scores + layer_scores(documents[:, 1, :], outgoing[:, 1, :])
    total = doc_rows * lax.axis_size("doc")
    mean = lax.psum(jnp.sum(scores, axis=0), "doc") / total
    centered = scores - mean
    var = lax.psum(jnp.sum(centered * centered, axis=0), "doc") / total
    return centered * lax.rsqrt(var + eps_var)


def solution(mesh):
    placed = (P("doc", None, None), P(("grp", "doc"), None, None), P(), P(), P())
    return jax.shard_map(
        shards, mesh=mesh, in_specs=placed, out_specs=P(("grp", "doc"), None), check_vma=False
    )
```

profile of v0, /device:TPU:2, one launch (start us, length us, event | category | flops | bytes accessed | tf_op | source)
XLA Modules:
  0.0 170.7 jit_solution(6107344138527427044)
XLA Ops:
  6.5 0.0 copy-start
  6.5 0.0 all-gather.7.cloned.1.call-start
  6.5 1.1 reshape.12
  7.7 0.9 reduce_sum.27
  8.6 0.9 broadcast_add_fusion
  9.6 0.0 copy-done
  9.6 0.4 convolution_bitcast_fusion.1
  10.0 1.8 %fusion.2 = f32[8,2,64,64]{3,2,0,1:T(8,128)S(1)} fusion(f32[8,2,64,64]{3,2,0,1:T(8,128)S(1)} %convolution_bitcast_fusion.1, f32[2,64,64]{2,1,0:T(8,128)S(1)} %broadcast_add_fusion, f32[2,64,64]{2,1,0:T(8,128)} %param.8), kind=kOutput, calls=%fused_computation.7 | convolution fusion | flops 50397184 | bytes 589824 | tf_op jit(solution)/shard_map/lai,qlab,lbj->qlij/dot_general | solution.py:19
  11.8 0.6 convolution_bitcast_fusion
  12.4 1.4 fusion.3
  13.9 0.3 convert_element_type.12
  14.1 0.7 fusion.13
  14.8 0.0 all-gather.7.cloned.1.call-update
  14.8 0.2 all-gather.5.cloned.1.call-start
  15.1 0.5 all-gather.5.cloned.1.call-update
  15.6 20.8 %fusion.12 = (bf16[512,1,4096]{2,1,0:T(2,128)(2,1)}, bf16[512,1,4096]{2,1,0:T(2,128)(2,1)}) fusion(bf16[512,2,4096]{2,1,0:T(2,128)(2,1)} %param.6), kind=kLoop, calls=%fused_computation.24 | loop fusion | bytes 16777216 | tf_op jit(solution)/shard_map/slice | solution.py:41
  36.4 17.7 %all-gather.7.cloned.1.call-done = bf16[128,1,4096]{2,0,1:T(8,128)(2,1)} async-done(((bf16[8,1,4096]{2,0,1:T(8,128)(2,1)}), bf16[128,1,4096]{2,0,1:T(8,128)(2,1)}) %all-gather.7.cloned.1.call-update) | async-done | bytes 1048592 | tf_op jit(solution)/shard_map/all_gather | solution.py:33
  54.1 8.3 %fusion = f32[128,512]{1,0:T(8,128)S(1)} fusion(bf16[512,1,4096]{2,1,0:T(2,128)(2,1)} %get-tuple-element.6, bf16[128,1,4096]{2,0,1:T(8,128)(2,1)} %all-gather.7.cloned.1.call-done), kind=kOutput, calls=%fused_computation.1 | convolution fusion | flops 536870912 | bytes 5505024 | tf_op jit(solution)/shard_map/dp,qp->dq/dot_general | solution.py:30
  62.5 30.7 %all-gather.5.cloned.1.call-done = bf16[128,1,4096]{2,0,1:T(8,128)(2,1)} async-done(((bf16[8,1,4096]{2,0,1:T(8,128)(2,1)}), bf16[128,1,4096]{2,0,1:T(8,128)(2,1)}) %all-gather.5.cloned.1.call-update) | async-done | bytes 1048592 | tf_op jit(solution)/shard_map/all_gather | solution.py:33
  93.2 8.4 %fusion.14 = (f32[128]{0:T(128)S(1)}, f32[128,512]{1,0:T(8,128)S(1)}) fusion(f32[128,512]{1,0:T(8,128)S(1)} %fusion, bf16[512,1,4096]{2,1,0:T(2,128)(2,1)} %get-tuple-element.5, bf16[128,1,4096]{2,0,1:T(8,128)(2,1)} %all-gather.5.cloned.1.call-done), kind=kOutput, calls=%fused_computation.26 | convolution fusion | flops 537001856 | bytes 5767680 | tf_op jit(solution)/shard_map/dp,qp->dq/dot_general | solution.py:30
  101.6 31.6 %psum.14 = f32[128]{0:T(128)S(1)} all-reduce(f32[128]{0:T(128)S(1)} %get-tuple-element.9), channel_id=1, replica_groups=mesh['grp'=2,'doc'=16] {'doc'}, use_global_device_ids=true, to_apply=%region_2.0 | all-reduce | flops 128 | bytes 1024 | tf_op jit(solution)/shard_map/psum | solution.py:44
  133.2 0.2 multiply_reduce_fusion
  133.4 29.5 %psum.15 = f32[128]{0:T(128)S(1)} all-reduce(f32[128]{0:T(128)S(1)} %multiply_reduce_fusion), channel_id=1, replica_groups=mesh['grp'=2,'doc'=16] {'doc'}, use_global_device_ids=true, to_apply=%region_4.0 | all-reduce | flops 128 | bytes 1024 | tf_op jit(solution)/shard_map/psum | solution.py:46
  162.9 0.1 multiply_bitcast_fusion
  163.0 0.8 copy.9
  (3 shorter events, 0.0 us)
Async XLA Ops:
  6.5 3.0 %copy-start = (f32[2,64,64]{2,1,0:T(8,128)S(1)}, f32[2,64,64]{2,1,0:T(8,128)}, u32[]{:S(2)}) copy-start(f32[2,64,64]{2,1,0:T(8,128)} %param.9) | copy-start | bytes 98308
  6.5 47.6 %all-gather.7.cloned.1.call-start = ((), (), s32[]{:S(2)}) async-start(), calls=%async_computation.1 | async-start | bytes 1114112 | tf_op jit(solution)/shard_map/all_gather | solution.py:33
  14.8 78.4 %all-gather.5.cloned.1.call-start = ((), (), s32[]{:S(2)}) async-start(), calls=%async_computation | async-start | bytes 1114112 | tf_op jit(solution)/shard_map/all_gather | solution.py:33
Sparse Core Ops, SparseCore 0:
  14.9 39.1 all-gather.6
  56.3 36.8 all-gather.4
where the time goes:
time: 173 us; the launch traced here: 171 us
  blocking collectives  61.1 us (35%)
  waiting for transfers between devices  49 us (28%)
  local copies, waits for them, and re-layouts  23.7 us (14%)
  matrix products  21 us (12%)
  between operations  13.5 us (8%)
  other arithmetic  2.17 us (1%)
    all_gather x2, waiting for transfers between devices, layer_scores(): lax.all_gather(query_layer, 'doc', axis=0, tiled=True)  48.5 us
    psum x1, blocking collectives, shards(): mean = lax.psum(jnp.sum(scores, axis=0), 'doc') / total  31.6 us
    psum x1, blocking collectives, shards(): var = lax.psum(jnp.sum(centered * centered, axis=0), 'doc') / total  29.5 us
    slice x2, local copies, waits for them, and re-layouts, shards(): scores = layer_scores(documents[:, 0, :], outgoing[:, 0, :])  21.5 us
    dot_general x2, matrix products, layer_scores(): jnp.einsum('dp,qp->dq', doc_layer, lax.all_gather(query_layer, 'doc', axi...  16.7 us
  transfers between devices with their start and end apart: 2, of which 2 were waited for; matrix products, arithmetic and copies ran while one was open for 17% of the time, Pallas kernels for 0%

commit v1 on v0

v1 whole, which is shorter than its diff:
```python
import functools

import jax
import jax.numpy as jnp
from jax import lax
from jax.experimental import pallas as pl
from jax.experimental.pallas import tpu as pltpu
from jax.sharding import PartitionSpec as P

SIDE = 64
damp_scale = 0.1
eps_var = 1e-06
F32 = jnp.float32
BF16 = jnp.bfloat16
MESH = pl.DeviceIdType.MESH
CHUNKS = 2
DOC_COPIES = 8


def flip(value, bits):
    at = 1
    while at <= bits:
        if bits & at:
            value = value + at - 2 * at * ((value // at) % 2)
        at *= 2
    return value


def split(x):
    hi = x.astype(BF16)
    return hi, (x - hi.astype(F32)).astype(BF16)


def dot3(a, b, dims):
    ah, al = a
    bh, bl = b
    dot = functools.partial(
        lax.dot_general, dimension_numbers=(dims, ((), ())), preferred_element_type=F32
    )
    total = dot(ah, bh) + dot(ah, bl)
    if al is not None:
        total = total + dot(al, bh)
    return total


def precondition(core, query_ref, eig_ref, in_ref, out_ref, wide, rows, put):
    lane = lax.broadcasted_iota(jnp.int32, (8, 128), 1)
    low = lane < SIDE
    for pair in range(SIDE // 2):
        wide[pair] = query_ref[:, pl.ds(pair * 128, 128)].astype(F32)
        first = wide[pair, pl.ds(0, 8, stride=2), :]
        second = wide[pair, pl.ds(1, 8, stride=2), :]
        rows[pl.ds(pair * 16, 8), :] = jnp.where(low, first, pltpu.roll(second, SIDE, 1))
        rows[pl.ds(pair * 16 + 8, 8), :] = jnp.where(low, pltpu.roll(first, SIDE, 1), second)

    zero = jnp.zeros((SIDE, SIDE), F32)
    diag = split(
        jnp.concatenate(
            [
                jnp.concatenate([in_ref[0], zero], axis=1),
                jnp.concatenate([zero, in_ref[1]], axis=1),
            ],
            axis=0,
        )
    )
    back_out = jnp.concatenate([out_ref[0], out_ref[1]], axis=0)
    fwd_out = split(jnp.concatenate([out_ref[0].T, out_ref[1].T], axis=0))
    back_out = split(back_out)
    inverse = []
    for layer in range(2):
        eig = eig_ref[layer]
        damping = damp_scale * (jnp.sum(eig) / (SIDE * SIDE))
        inverse.append(1.0 / (eig + damping))
    inverse = jnp.concatenate(inverse, axis=1)

    rows[...] = dot3((rows[...].astype(BF16), None), diag, ((1,), (0,)))
    by_a = jnp.concatenate([rows[pl.ds(q, SIDE, stride=8), :] for q in range(8)], axis=1)
    own = lax.broadcasted_iota(jnp.int32, (SIDE, 128), 1) < SIDE
    own = jnp.concatenate([own.astype(F32)] * 8, axis=1) > 0.5
    both = dot3(fwd_out, split(by_a), ((1,), (0,)))
    scaled = jnp.where(own, both[:SIDE], both[SIDE:]) * jnp.concatenate([inverse] * 8, axis=1)
    both = dot3(back_out, split(scaled), ((1,), (0,)))
    back = jnp.where(own, both[:SIDE], both[SIDE:])
    for q in range(8):
        rows[pl.ds(q, SIDE, stride=8), :] = back[:, q * 128 : (q + 1) * 128]
    rows[...] = dot3(split(rows[...]), diag, ((1,), (1,)))

    swap = core == 1
    for pair in range(SIDE // 2):
        even = rows[pl.ds(pair * 16, 8), :]
        odd = rows[pl.ds(pair * 16 + 8, 8), :]
        one = jnp.where(low, even, pltpu.roll(odd, SIDE, 1))
        two = jnp.where(low, pltpu.roll(even, SIDE, 1), odd)
        upper = jnp.where(swap, two, one)
        lower = jnp.where(swap, one, two)
        put(pair, jnp.concatenate([upper, lower], axis=0).astype(BF16))


def kernel(
    n, query_ref, docs_ref, eig_ref, in_ref, out_basis_ref, result_ref,
    docs, gathered, acc, score, wide, rows, stats,
    doc_sem, send_sem, recv_sem, stat_send, stat_recv,
):
    depth = n // 4
    grp = lax.axis_index("grp")
    me = lax.axis_index("doc")
    other = flip(grp, 1)
    z, y, core = me // 4, (me // 2) % 2, me % 2
    leads = core == grp % 2
    beside, sibling = flip(me, 2), flip(me, 1)

    doc_rows = docs.shape[0]
    part = doc_rows // DOC_COPIES
    flat = docs_ref.reshape(doc_rows, docs.shape[1])
    loads = [
        pltpu.make_async_copy(
            flat.at[pl.ds(i * part, part), :], docs.at[pl.ds(i * part, part), :], doc_sem.at[i]
        )
        for i in range(DOC_COPIES)
    ]

    barrier = pltpu.get_barrier_semaphore()
    for k in range(1, n):
        pl.semaphore_signal(
            barrier, inc=1, device_id=(grp, lax.rem(me + k, n)), device_id_type=MESH
        )
    pl.semaphore_signal(barrier, inc=1, device_id=(other, me), device_id_type=MESH)
    for load in loads:
        load.start()

    def slot(plane, row, c):
        return c * (n // 2) + plane * 2 + row

    mine = slot(z, y, core)

    def put(pair, block):
        gathered[mine, :, pl.ds(pair * 128, 128)] = block

    precondition(core, query_ref, eig_ref, in_ref, out_basis_ref, wide, rows, put)
    pl.semaphore_wait(barrier, n)

    width = gathered.shape[2] // CHUNKS
    half = width // 2
    used = [0]
    lead_sends, follow_sends, all_sends = [], [], []

    def copy(where, block, chunk, piece, device):
        start = chunk * width + (half if piece == 1 else 0)
        ref = gathered.at[block, :, pl.ds(start, width if piece is None else half)]
        made = pltpu.make_async_remote_copy(
            src_ref=ref,
            dst_ref=ref,
            send_sem=send_sem.at[used[0]],
            recv_sem=recv_sem.at[block, chunk, 1 if piece == 1 else 0],
            device_id=device,
            device_id_type=MESH,
        )
        used[0] += 1
        made.start()
        where.append(made)

    def arrived(block, chunk, piece):
        start = chunk * width + (half if piece == 1 else 0)
        ref = gathered.at[block, :, pl.ds(start, width if piece is None else half)]
        pltpu.make_async_remote_copy(
            src_ref=ref,
            dst_ref=ref,
            send_sem=send_sem.at[0],
            recv_sem=recv_sem.at[block, chunk, 1 if piece == 1 else 0],
            device_id=(grp, sibling),
            device_id_type=MESH,
        ).wait_recv()

    to_beside, to_other, to_sibling = (grp, beside), (other, me), (grp, sibling)

    @pl.when(leads)
    def _():
        sends = lead_sends
        for chunk in range(CHUNKS):
            copy(sends, mine, chunk, None, to_beside)
            for step in range(1, depth):
                copy(sends, mine, chunk, None, (grp, flip(z, step) * 4 + me % 4))
            copy(sends, mine, chunk, None, to_sibling)

        def near(step, chunk):
            block = slot(flip(z, step), y, core)
            arrived(block, chunk, None)
            copy(sends, block, chunk, None, to_other)
            copy(sends, block, chunk, None, to_beside)
            copy(sends, block, chunk, None, to_sibling)

        def far(step, chunk):
            block = slot(flip(z, step), 1 - y, core)
            arrived(block, chunk, None)
            copy(sends, block, chunk, 0, to_other)
            copy(sends, block, chunk, None, to_sibling)

        for chunk in range(CHUNKS):
            for step in range(1, depth):
                near(step, chunk)
                far(step - 1, chunk)
            far(depth - 1, chunk)
        for made in sends:
            made.wait_send()

    lead_used, used[0] = used[0], 0

    @pl.when(jnp.logical_not(leads))
    def _():
        sends = follow_sends
        for chunk in range(CHUNKS):
            copy(sends, mine, chunk, 1, to_beside)
            copy(sends, mine, chunk, None, to_sibling)

        def near(step, chunk):
            block = slot(flip(z, step), y, core)
            arrived(block, chunk, None)
            copy(sends, block, chunk, 1, to_beside)
            copy(sends, block, chunk, None, to_sibling)

        def far(step, chunk):
            block = slot(flip(z, step), 1 - y, core)
            for piece in (1, 0):
                arrived(block, chunk, piece)
            copy(sends, block, chunk, None, to_sibling)

        for chunk in range(CHUNKS):
            for step in range(1, depth):
                near(step, chunk)
                far(step - 1, chunk)
            far(depth - 1, chunk)
        for made in sends:
            made.wait_send()

    for chunk in range(CHUNKS):
        for step in range(depth):
            arrived(slot(flip(z, step), y, 1 - core), chunk, None)
            arrived(slot(flip(z, step), 1 - y, 1 - core), chunk, None)
    for load in loads:
        load.wait()

    lanes = n * 8
    for chunk in range(CHUNKS):
        cols = pl.ds(chunk * width, width)
        right = gathered[:, :, cols].reshape(n * 16, width)
        product = lax.dot_general(
            docs[:, cols], right, (((1,), (1,)), ((), ())), preferred_element_type=F32
        )
        for tile in range(n // 8):
            piece = product[:, tile * 128 : (tile + 1) * 128]
            acc[tile] = piece if chunk == 0 else acc[tile] + piece

    count = doc_rows // 2
    for at in range(0, lanes, 128):
        upper = lax.broadcasted_iota(jnp.int32, (count, 128), 1) // 8 % 2 == 0
        even, odd = pl.ds(0, count, stride=2), pl.ds(1, count, stride=2)
        first, second = at // 128, (lanes + at) // 128
        direct = jnp.where(upper, acc[first, even, :], acc[second, even, :])
        cross = jnp.where(upper, acc[second, odd, :], acc[first, odd, :])
        cross = jnp.where(upper, pltpu.roll(cross, 120, 1), pltpu.roll(cross, 8, 1))
        score[:, pl.ds(at, 128)] = direct + cross

    values = score[...]
    local_mean = jnp.sum(values, axis=0, keepdims=True) / count
    away = values - local_mean
    spread = jnp.sum(away * away, axis=0, keepdims=True)
    row = lax.broadcasted_iota(jnp.int32, (8, lanes), 0)
    stats[me] = jnp.where(row == 0, local_mean, spread)
    shares = []
    for k in range(1, n):
        share = pltpu.make_async_remote_copy(
            src_ref=stats.at[me],
            dst_ref=stats.at[me],
            send_sem=stat_send.at[k],
            recv_sem=stat_recv.at[k],
            device_id=(grp, lax.rem(me + k, n)),
            device_id_type=MESH,
        )
        share.start()
        shares.append(share)
    for k in range(1, n):
        source = lax.rem(me + n - k, n)
        pltpu.make_async_remote_copy(
            src_ref=stats.at[me],
            dst_ref=stats.at[source],
            send_sem=stat_send.at[k],
            recv_sem=stat_recv.at[k],
            device_id=(grp, source),
            device_id_type=MESH,
        ).wait_recv()
    for share in shares:
        share.wait_send()
    merged = stats[...]
    means, spreads = merged[:, 0:1, :], merged[:, 1:2, :]
    mean = jnp.sum(means, axis=0) / n
    shift = means - mean[None]
    var = (jnp.sum(spreads, axis=0) + count * jnp.sum(shift * shift, axis=0)) / (count * n)
    result_ref[...] = (values - mean) * lax.rsqrt(var + eps_var)


def shards(queries, documents, eigvals, basis_in, basis_out):
    n = lax.axis_size("doc")
    doc_rows, layers, proj = documents.shape
    vmem = pl.BlockSpec(memory_space=pltpu.VMEM)
    queries = queries.reshape(queries.shape[0] * layers, proj)
    most = CHUNKS * (6 * (n // 4) + 4)
    return pl.pallas_call(
        functools.partial(kernel, n),
        out_shape=jax.ShapeDtypeStruct((doc_rows, n * 8), F32),
        in_specs=[vmem, pl.BlockSpec(memory_space=pl.ANY), vmem, vmem, vmem],
        out_specs=vmem,
        scratch_shapes=[
            pltpu.VMEM((doc_rows * layers, proj), BF16),
            pltpu.VMEM((n, 16, proj), BF16),
            pltpu.VMEM((n // 8, doc_rows * layers, 128), F32),
            pltpu.VMEM((doc_rows, n * 8), F32),
            pltpu.VMEM((proj // 128, 16, 128), F32),
            pltpu.VMEM((8 * SIDE, 128), F32),
            pltpu.VMEM((n, 8, n * 8), F32),
            pltpu.SemaphoreType.DMA((DOC_COPIES,)),
            pltpu.SemaphoreType.DMA((most,)),
            pltpu.SemaphoreType.DMA((n, CHUNKS, 2)),
            pltpu.SemaphoreType.DMA((n,)),
            pltpu.SemaphoreType.DMA((n,)),
        ],
        compiler_params=pltpu.CompilerParams(
            collective_id=0, has_side_effects=True, vmem_limit_bytes=56 * 1024 * 1024
        ),
        cost_estimate=pl.CostEstimate(
            flops=2 * doc_rows * layers * proj * n * 16,
            bytes_accessed=2 * doc_rows * layers * proj,
            transcendentals=0,
        ),
    )(queries, documents, eigvals, basis_in, basis_out)


def solution(mesh):
    placed = (P("doc", None, None), P(("grp", "doc"), None, None), P(), P(), P())
    return jax.shard_map(
        shards, mesh=mesh, in_specs=placed, out_specs=P(("grp", "doc"), None), check_vma=False
    )
```

time: 173 us -> 37.9 us (0.22); the launches traced: 171 us -> 37.4 us
  blocking collectives: 61.1 us -> 0 us
  waiting for transfers between devices: 49 us -> 0 us
  Pallas kernels: 0 us -> 34.1 us
  matrix products: 21 us -> 0 us
  local copies, waits for them, and re-layouts: 23.7 us -> 3.28 us
  between operations: 13.5 us -> 0.01 us
  other arithmetic: 2.17 us -> 0 us
    psum x2 -> x0, blocking collectives: 61.1 us -> none  [the longest x1 31.6 us: shards(): mean = lax.psum(jnp.sum(scores, axis=0), 'doc') / total]
    all_gather x2 -> x0, waiting for transfers between devices: 48.5 us -> none  [layer_scores(): lax.all_gather(query_layer, 'doc', axis=0, tiled=True)]
    pallas_call x0 -> x1, Pallas kernels: none -> 34.1 us  [shards(): pl.pallas_call(functools.partial(kernel, n), out_shape=jax.ShapeDtypeStru...]
    slice x2 -> x0, local copies, waits for them, and re-layouts: 21.5 us -> none  [shards(): scores = layer_scores(documents[:, 0, :], outgoing[:, 0, :])]
    dot_general x6 -> x0, matrix products: 21 us -> none  [the longest x2 16.7 us: layer_scores(): jnp.einsum('dp,qp->dq', doc_layer, lax.all_gather(query_layer, 'doc', axi...]
  transfers between devices with their start and end apart: 2 -> 0, of which waited for: 2 -> 0; matrix products, arithmetic and copies ran while one was open for 17% -> 0% of each run, Pallas kernels for 0% -> 0%
where the time goes in v1:
time: 37.9 us; the launch traced here: 37.4 us
  Pallas kernels  34.1 us (90%)
  local copies, waits for them, and re-layouts  3.28 us (9%)
    pallas_call x1, Pallas kernels, shards(): pl.pallas_call(functools.partial(kernel, n), out_shape=jax.ShapeDtypeStru...  34.1 us
    unnamed x1, local copies, waits for them, and re-layouts  1.67 us
    reshape x1, local copies, waits for them, and re-layouts, shards(): queries = queries.reshape(queries.shape[0] * layers, proj)  1.61 us

profile of v1, /device:TPU:2, one launch (start us, length us, event | category | flops | bytes accessed | tf_op | source)
XLA Modules:
  0.0 37.4 jit_solution(4436367058025864073)
XLA Ops:
  0.0 1.6 %reshape.3.query_ref = bf16[16,4096]{1,0:T(8,128)(2,1)} reshape(bf16[8,2,4096]{2,1,0:T(2,128)(2,1)} %param.5) | data formatting | bytes 262144 | tf_op jit(solution)/shard_map/reshape | solution.py:305
  1.6 34.1 %shard_map.55 = f32[512,128]{1,0:T(8,128)} custom-call(bf16[16,4096]{1,0:T(8,128)(2,1)} %reshape.3.query_ref, bf16[512,2,4096]{2,1,0:T(2,128)(2,1)} %docs_ref.1, f32[2,64,64]{2,1,0:T(8,128)} %eig_ref.1, f32[2,64,64]{2,1,0:T(8,128)} %in_ref.1, f32[2,64,64]{2,1,0:T(8,128)} %out_basis_ref.1), custom_call_target="tpu_custom_call" | custom-call | flops 2147483648 | bytes 8388608 | tf_op jit(solution)/shard_map/pallas_call | solution.py:307
  35.7 1.7 %copy.7 = f32[512,128]{1,0:T(8,128)} copy(f32[512,128]{1,0:T(8,128)} %shard_map.55) | data formatting | bytes 524288

commit v2 on v1

--- a/solution.py
+++ b/solution.py
@@ -14,6 +14,7 @@
 BF16 = jnp.bfloat16
 MESH = pl.DeviceIdType.MESH
 CHUNKS = 2
+LAG = 1
 DOC_COPIES = 8
 
 
@@ -98,7 +99,7 @@
 
 def kernel(
     n, query_ref, docs_ref, eig_ref, in_ref, out_basis_ref, result_ref,
-    docs, gathered, acc, score, wide, rows, stats,
+    query, docs, gathered, acc, score, wide, rows, stats,
     doc_sem, send_sem, recv_sem, stat_send, stat_recv,
 ):
     depth = n // 4
@@ -119,12 +120,15 @@
         for i in range(DOC_COPIES)
     ]
 
+    fetch = pltpu.make_async_copy(
+        query_ref.reshape(16, docs.shape[1]), query, doc_sem.at[DOC_COPIES]
+    )
+    fetch.start()
     barrier = pltpu.get_barrier_semaphore()
-    for k in range(1, n):
-        pl.semaphore_signal(
-            barrier, inc=1, device_id=(grp, lax.rem(me + k, n)), device_id_type=MESH
-        )
-    pl.semaphore_signal(barrier, inc=1, device_id=(other, me), device_id_type=MESH)
+    plane_peers = [(grp, flip(me, bits)) for bits in (1, 2, 3)]
+    column_peers = [(grp, lax.rem(me + 4 * k, n)) for k in range(1, depth)]
+    for peer in plane_peers + column_peers + [(other, me)]:
+        pl.semaphore_signal(barrier, inc=1, device_id=peer, device_id_type=MESH)
     for load in loads:
         load.start()
 
@@ -136,106 +140,140 @@
     def put(pair, block):
         gathered[mine, :, pl.ds(pair * 128, 128)] = block
 
-    precondition(core, query_ref, eig_ref, in_ref, out_basis_ref, wide, rows, put)
-    pl.semaphore_wait(barrier, n)
+    fetch.wait()
+    precondition(core, query, eig_ref, in_ref, out_basis_ref, wide, rows, put)
+    pl.semaphore_wait(barrier, depth + 3)
 
     width = gathered.shape[2] // CHUNKS
     half = width // 2
-    used = [0]
-    lead_sends, follow_sends, all_sends = [], [], []
-
-    def copy(where, block, chunk, piece, device):
+    pending = []
+
+    def columns(chunk, piece):
         start = chunk * width + (half if piece == 1 else 0)
-        ref = gathered.at[block, :, pl.ds(start, width if piece is None else half)]
+        return pl.ds(start, width if piece is None else half)
+
+    def guard(condition, body):
+        pl.when(condition())(body) if condition else body()
+
+    def copy(block, chunk, piece, device, condition=None):
+        ref = gathered.at[block, :, columns(chunk, piece)]
         made = pltpu.make_async_remote_copy(
             src_ref=ref,
             dst_ref=ref,
-            send_sem=send_sem.at[used[0]],
+            send_sem=send_sem.at[len(pending)],
             recv_sem=recv_sem.at[block, chunk, 1 if piece == 1 else 0],
             device_id=device,
             device_id_type=MESH,
         )
-        used[0] += 1
         made.start()
-        where.append(made)
-
-    def arrived(block, chunk, piece):
-        start = chunk * width + (half if piece == 1 else 0)
-        ref = gathered.at[block, :, pl.ds(start, width if piece is None else half)]
-        pltpu.make_async_remote_copy(
+        pending.append((piece, condition))
+
+    def wait_for(block, chunk, piece, sends=None):
+        ref = gathered.at[block, :, columns(chunk, piece)]
+        made = pltpu.make_async_remote_copy(
             src_ref=ref,
             dst_ref=ref,
-            send_sem=send_sem.at[0],
+            send_sem=send_sem.at[sends or 0],
             recv_sem=recv_sem.at[block, chunk, 1 if piece == 1 else 0],
             device_id=(grp, sibling),
             device_id_type=MESH,
-        ).wait_recv()
+        )
+        made.wait_recv() if sends is None else made.wait_send()
+
+    def drain():
+        for at, (piece, condition) in enumerate(pending):
+            guard(condition, functools.partial(wait_for, mine, 0, piece, at))
+        pending.clear()
 
     to_beside, to_other, to_sibling = (grp, beside), (other, me), (grp, sibling)
+
+    def planes(dist):
+        if dist == 0:
+            return [
+                (z, 1, None, lambda: z + 1 < depth),
+                (z, -1, None, lambda: z >= 1),
+            ]
+        return [
+            (z - dist, 1, lambda: z >= dist,
+             lambda: jnp.logical_and(z >= dist, z + 1 < depth)),
+            (z + dist, -1, lambda: z + dist < depth,
+             lambda: jnp.logical_and(z + dist < depth, z >= 1)),
+        ]
+
+    def lead_near(dist, chunk):
+        for plane, step, there, further in planes(dist):
+            block = slot(plane, y, core)
+
+            def onward():
+                copy(block, chunk, None, (grp, me + 4 * step), further)
+
+            def spread():
+                copy(block, chunk, None, to_beside, there)
+                if dist:
+                    copy(block, chunk, None, to_other, there)
+                copy(block, chunk, None, to_sibling, there)
+
+            if dist:
+                guard(there, functools.partial(wait_for, block, chunk, None))
+            guard(further, onward)
+            if dist or step < 0:
+                guard(there, spread)
+
+    def lead_far(dist, chunk):
+        for plane, _, there, _ in planes(dist)[: 2 if dist else 1]:
+            block = slot(plane, 1 - y, core)
+
+            def spread():
+                wait_for(block, chunk, None)
+                copy(block, chunk, 0, to_other, there)
+                copy(block, chunk, None, to_sibling, there)
+
+            guard(there, spread)
+
+    def follow_near(dist, chunk):
+        for plane, _, there, _ in planes(dist)[: 2 if dist else 1]:
+            block = slot(plane, y, core)
+
+            def spread():
+                if dist:
+                    wait_for(block, chunk, None)
+                copy(block, chunk, 1, to_beside, there)
+                copy(block, chunk, None, to_sibling, there)
+
+            guard(there, spread)
+
+    def follow_far(dist, chunk):
+        for plane, _, there, _ in planes(dist)[: 2 if dist else 1]:
+            block = slot(plane, 1 - y, core)
+
+            def spread():
+                wait_for(block, chunk, 1)
+                wait_for(block, chunk, 0)
+                copy(block, chunk, None, to_sibling, there)
+
+            guard(there, spread)
+
+    def walk(near, far):
+        for dist in range(depth + LAG):
+            for chunk in range(CHUNKS):
+                if dist < depth:
+                    near(dist, chunk)
+                if dist >= LAG:
+                    far(dist - LAG, chunk)
+        drain()
 
     @pl.when(leads)
     def _():
-        sends = lead_sends
-        for chunk in range(CHUNKS):
-            copy(sends, mine, chunk, None, to_beside)
-            for step in range(1, depth):
-                copy(sends, mine, chunk, None, (grp, flip(z, step) * 4 + me % 4))
-            copy(sends, mine, chunk, None, to_sibling)
-
-        def near(step, chunk):
-            block = slot(flip(z, step), y, core)
-            arrived(block, chunk, None)
-            copy(sends, block, chunk, None, to_other)
-            copy(sends, block, chunk, None, to_beside)
-            copy(sends, block, chunk, None, to_sibling)
-
-        def far(step, chunk):
-            block = slot(flip(z, step), 1 - y, core)
-            arrived(block, chunk, None)
-            copy(sends, block, chunk, 0, to_other)
-            copy(sends, block, chunk, None, to_sibling)
-
-        for chunk in range(CHUNKS):
-            for step in range(1, depth):
-                near(step, chunk)
-                far(step - 1, chunk)
-            far(depth - 1, chunk)
-        for made in sends:
-            made.wait_send()
-
-    lead_used, used[0] = used[0], 0
+        walk(lead_near, lead_far)
 
     @pl.when(jnp.logical_not(leads))
     def _():
-        sends = follow_sends
-        for chunk in range(CHUNKS):
-            copy(sends, mine, chunk, 1, to_beside)
-            copy(sends, mine, chunk, None, to_sibling)
-
-        def near(step, chunk):
-            block = slot(flip(z, step), y, core)
-            arrived(block, chunk, None)
-            copy(sends, block, chunk, 1, to_beside)
-            copy(sends, block, chunk, None, to_sibling)
-
-        def far(step, chunk):
-            block = slot(flip(z, step), 1 - y, core)
-            for piece in (1, 0):
-                arrived(block, chunk, piece)
-            copy(sends, block, chunk, None, to_sibling)
-
-        for chunk in range(CHUNKS):
-            for step in range(1, depth):
-                near(step, chunk)
-                far(step - 1, chunk)
-            far(depth - 1, chunk)
-        for made in sends:
-            made.wait_send()
+        walk(follow_near, follow_far)
 
     for chunk in range(CHUNKS):
         for step in range(depth):
-            arrived(slot(flip(z, step), y, 1 - core), chunk, None)
-            arrived(slot(flip(z, step), 1 - y, 1 - core), chunk, None)
+            wait_for(slot(step, y, 1 - core), chunk, None)
+            wait_for(slot(step, 1 - y, 1 - core), chunk, None)
     for load in loads:
         load.wait()
 
@@ -265,36 +303,33 @@
     away = values - local_mean
     spread = jnp.sum(away * away, axis=0, keepdims=True)
     row = lax.broadcasted_iota(jnp.int32, (8, lanes), 0)
-    stats[me] = jnp.where(row == 0, local_mean, spread)
-    shares = []
-    for k in range(1, n):
-        share = pltpu.make_async_remote_copy(
-            src_ref=stats.at[me],
-            dst_ref=stats.at[me],
-            send_sem=stat_send.at[k],
-            recv_sem=stat_recv.at[k],
-            device_id=(grp, lax.rem(me + k, n)),
-            device_id_type=MESH,
-        )
-        share.start()
-        shares.append(share)
-    for k in range(1, n):
-        source = lax.rem(me + n - k, n)
-        pltpu.make_async_remote_copy(
-            src_ref=stats.at[me],
-            dst_ref=stats.at[source],
-            send_sem=stat_send.at[k],
-            recv_sem=stat_recv.at[k],
-            device_id=(grp, source),
-            device_id_type=MESH,
-        ).wait_recv()
-    for share in shares:
-        share.wait_send()
-    merged = stats[...]
-    means, spreads = merged[:, 0:1, :], merged[:, 1:2, :]
-    mean = jnp.sum(means, axis=0) / n
-    shift = means - mean[None]
-    var = (jnp.sum(spreads, axis=0) + count * jnp.sum(shift * shift, axis=0)) / (count * n)
+
+    def merge(members, weight, mean, spread, first):
+        stats[first] = jnp.where(row == 0, mean, spread)
+        shares = []
+        for at, peer in enumerate(members):
+            share = pltpu.make_async_remote_copy(
+                src_ref=stats.at[first],
+                dst_ref=stats.at[first + 1 + at],
+                send_sem=stat_send.at[first + at],
+                recv_sem=stat_recv.at[first + at],
+                device_id=peer,
+                device_id_type=MESH,
+            )
+            share.start()
+            shares.append(share)
+        for share in shares:
+            share.wait()
+        total = len(members) + 1
+        merged = [stats[first + at] for at in range(total)]
+        middle = sum(part[0:1] for part in merged) / total
+        wide_spread = sum(part[1:2] for part in merged)
+        shift = sum((part[0:1] - middle) * (part[0:1] - middle) for part in merged)
+        return middle, wide_spread + weight * shift
+
+    mean, spread = merge(plane_peers, count, local_mean, spread, 0)
+    mean, spread = merge(column_peers, count * 4, mean, spread, 4)
+    var = spread / (count * n)
     result_ref[...] = (values - mean) * lax.rsqrt(var + eps_var)
 
 
@@ -302,22 +337,22 @@
     n = lax.axis_size("doc")
     doc_rows, layers, proj = documents.shape
     vmem = pl.BlockSpec(memory_space=pltpu.VMEM)
-    queries = queries.reshape(queries.shape[0] * layers, proj)
-    most = CHUNKS * (6 * (n // 4) + 4)
+    most = CHUNKS * (12 * (n // 4))
     return pl.pallas_call(
         functools.partial(kernel, n),
         out_shape=jax.ShapeDtypeStruct((doc_rows, n * 8), F32),
-        in_specs=[vmem, pl.BlockSpec(memory_space=pl.ANY), vmem, vmem, vmem],
+        in_specs=[pl.BlockSpec(memory_space=pl.ANY)] * 2 + [vmem] * 3,
         out_specs=vmem,
         scratch_shapes=[
+            pltpu.VMEM((16, proj), BF16),
             pltpu.VMEM((doc_rows * layers, proj), BF16),
             pltpu.VMEM((n, 16, proj), BF16),
             pltpu.VMEM((n // 8, doc_rows * layers, 128), F32),
             pltpu.VMEM((doc_rows, n * 8), F32),
             pltpu.VMEM((proj // 128, 16, 128), F32),
             pltpu.VMEM((8 * SIDE, 128), F32),
-            pltpu.VMEM((n, 8, n * 8), F32),
-            pltpu.SemaphoreType.DMA((DOC_COPIES,)),
+            pltpu.VMEM((4 + n // 4, 8, n * 8), F32),
+            pltpu.SemaphoreType.DMA((DOC_COPIES + 1,)),
             pltpu.SemaphoreType.DMA((most,)),
             pltpu.SemaphoreType.DMA((n, CHUNKS, 2)),
             pltpu.SemaphoreType.DMA((n,)),

time: 37.9 us -> 35.8 us (0.945)
  local copies, waits for them, and re-layouts: 3.28 us -> 1.67 us
    reshape x1 -> x0, local copies, waits for them, and re-layouts: 1.61 us -> none  [shards(): queries = queries.reshape(queries.shape[0] * layers, proj)]
where the time goes in v2:
time: 35.8 us; the launch traced here: 35.6 us
  Pallas kernels  33.9 us (95%)
  local copies, waits for them, and re-layouts  1.67 us (5%)
    pallas_call x1, Pallas kernels, shards(): pl.pallas_call(functools.partial(kernel, n), out_shape=jax.ShapeDtypeStru...  33.9 us
    unnamed x1, local copies, waits for them, and re-layouts  1.67 us

profile of v2, /device:TPU:2, one launch (start us, length us, event | category | flops | bytes accessed | tf_op | source)
XLA Modules:
  0.0 35.6 jit_solution(9504889210563884830)
XLA Ops:
  0.0 33.9 %shard_map.55 = f32[512,128]{1,0:T(8,128)} custom-call(bf16[8,2,4096]{2,1,0:T(2,128)(2,1)} %query_ref.1, bf16[512,2,4096]{2,1,0:T(2,128)(2,1)} %docs_ref.1, f32[2,64,64]{2,1,0:T(8,128)} %eig_ref.1, f32[2,64,64]{2,1,0:T(8,128)} %in_ref.1, f32[2,64,64]{2,1,0:T(8,128)} %out_basis_ref.1), custom_call_target="tpu_custom_call" | custom-call | flops 2147483648 | bytes 8388608 | tf_op jit(solution)/shard_map/pallas_call | solution.py:341
  33.9 1.7 %copy.7 = f32[512,128]{1,0:T(8,128)} copy(f32[512,128]{1,0:T(8,128)} %shard_map.55) | data formatting | bytes 524288

commit v3 on v2

--- a/solution.py
+++ b/solution.py
@@ -125,9 +125,7 @@
     )
     fetch.start()
     barrier = pltpu.get_barrier_semaphore()
-    plane_peers = [(grp, flip(me, bits)) for bits in (1, 2, 3)]
-    column_peers = [(grp, lax.rem(me + 4 * k, n)) for k in range(1, depth)]
-    for peer in plane_peers + column_peers + [(other, me)]:
+    for peer in [(grp, lax.rem(me + k, n)) for k in range(1, n)] + [(other, me)]:
         pl.semaphore_signal(barrier, inc=1, device_id=peer, device_id_type=MESH)
     for load in loads:
         load.start()
@@ -142,7 +140,7 @@
 
     fetch.wait()
     precondition(core, query, eig_ref, in_ref, out_basis_ref, wide, rows, put)
-    pl.semaphore_wait(barrier, depth + 3)
+    pl.semaphore_wait(barrier, n)
 
     width = gathered.shape[2] // CHUNKS
     half = width // 2
@@ -188,39 +186,33 @@
     to_beside, to_other, to_sibling = (grp, beside), (other, me), (grp, sibling)
 
     def planes(dist):
+        below, above = (lambda: z >= dist), (lambda: z + dist < depth)
         if dist == 0:
-            return [
-                (z, 1, None, lambda: z + 1 < depth),
-                (z, -1, None, lambda: z >= 1),
-            ]
-        return [
-            (z - dist, 1, lambda: z >= dist,
-             lambda: jnp.logical_and(z >= dist, z + 1 < depth)),
-            (z + dist, -1, lambda: z + dist < depth,
-             lambda: jnp.logical_and(z + dist < depth, z >= 1)),
-        ]
+            return [(z, 1, None, None)]
+        return [(z - dist, 1, below, above), (z + dist, -1, above, below)]
 
     def lead_near(dist, chunk):
-        for plane, step, there, further in planes(dist):
+        if dist == 0:
+            copy(mine, chunk, None, to_beside)
+            for hops in range(1, depth):
+                for _, step, _, there in planes(hops):
+                    target = (grp, me + 4 * step * hops)
+                    guard(there, functools.partial(copy, mine, chunk, None, target, there))
+            copy(mine, chunk, None, to_sibling)
+            return
+        for plane, _, there, _ in planes(dist):
             block = slot(plane, y, core)
 
-            def onward():
-                copy(block, chunk, None, (grp, me + 4 * step), further)
-
             def spread():
+                wait_for(block, chunk, None)
+                copy(block, chunk, None, to_other, there)
                 copy(block, chunk, None, to_beside, there)
-                if dist:
-                    copy(block, chunk, None, to_other, there)
                 copy(block, chunk, None, to_sibling, there)
 
-            if dist:
-                guard(there, functools.partial(wait_for, block, chunk, None))
-            guard(further, onward)
-            if dist or step < 0:
-                guard(there, spread)
+            guard(there, spread)
 
     def lead_far(dist, chunk):
-        for plane, _, there, _ in planes(dist)[: 2 if dist else 1]:
+        for plane, _, there, _ in planes(dist):
             block = slot(plane, 1 - y, core)
 
             def spread():
@@ -231,7 +223,7 @@
             guard(there, spread)
 
     def follow_near(dist, chunk):
-        for plane, _, there, _ in planes(dist)[: 2 if dist else 1]:
+        for plane, _, there, _ in planes(dist):
             block = slot(plane, y, core)
 
             def spread():
@@ -243,7 +235,7 @@
             guard(there, spread)
 
     def follow_far(dist, chunk):
-        for plane, _, there, _ in planes(dist)[: 2 if dist else 1]:
+        for plane, _, there, _ in planes(dist):
             block = slot(plane, 1 - y, core)
 
             def spread():
@@ -304,32 +296,36 @@
     spread = jnp.sum(away * away, axis=0, keepdims=True)
     row = lax.broadcasted_iota(jnp.int32, (8, lanes), 0)
 
-    def merge(members, weight, mean, spread, first):
-        stats[first] = jnp.where(row == 0, mean, spread)
-        shares = []
-        for at, peer in enumerate(members):
-            share = pltpu.make_async_remote_copy(
-                src_ref=stats.at[first],
-                dst_ref=stats.at[first + 1 + at],
-                send_sem=stat_send.at[first + at],
-                recv_sem=stat_recv.at[first + at],
-                device_id=peer,
-                device_id_type=MESH,
-            )
-            share.start()
-            shares.append(share)
-        for share in shares:
-            share.wait()
-        total = len(members) + 1
-        merged = [stats[first + at] for at in range(total)]
-        middle = sum(part[0:1] for part in merged) / total
-        wide_spread = sum(part[1:2] for part in merged)
-        shift = sum((part[0:1] - middle) * (part[0:1] - middle) for part in merged)
-        return middle, wide_spread + weight * shift
-
-    mean, spread = merge(plane_peers, count, local_mean, spread, 0)
-    mean, spread = merge(column_peers, count * 4, mean, spread, 4)
-    var = spread / (count * n)
+    stats[me] = jnp.where(row == 0, local_mean, spread)
+    shares = []
+    for k in range(1, n):
+        share = pltpu.make_async_remote_copy(
+            src_ref=stats.at[me],
+            dst_ref=stats.at[me],
+            send_sem=stat_send.at[k],
+            recv_sem=stat_recv.at[k],
+            device_id=(grp, lax.rem(me + k, n)),
+            device_id_type=MESH,
+        )
+        share.start()
+        shares.append(share)
+    for k in range(1, n):
+        source = lax.rem(me + n - k, n)
+        pltpu.make_async_remote_copy(
+            src_ref=stats.at[me],
+            dst_ref=stats.at[source],
+            send_sem=stat_send.at[k],
+            recv_sem=stat_recv.at[k],
+            device_id=(grp, source),
+            device_id_type=MESH,
+        ).wait_recv()
+    for share in shares:
+        share.wait_send()
+    merged = stats[...]
+    means, spreads = merged[:, 0:1, :], merged[:, 1:2, :]
+    mean = jnp.sum(means, axis=0) / n
+    shift = means - mean[None]
+    var = (jnp.sum(spreads, axis=0) + count * jnp.sum(shift * shift, axis=0)) / (count * n)
     result_ref[...] = (values - mean) * lax.rsqrt(var + eps_var)
 
 
@@ -351,7 +347,7 @@
             pltpu.VMEM((doc_rows, n * 8), F32),
             pltpu.VMEM((proj // 128, 16, 128), F32),
             pltpu.VMEM((8 * SIDE, 128), F32),
-            pltpu.VMEM((4 + n // 4, 8, n * 8), F32),
+            pltpu.VMEM((n, 8, n * 8), F32),
             pltpu.SemaphoreType.DMA((DOC_COPIES + 1,)),
             pltpu.SemaphoreType.DMA((most,)),
             pltpu.SemaphoreType.DMA((n, CHUNKS, 2)),

time: 35.8 us -> 33.7 us (0.941)
  Pallas kernels: 33.9 us -> 31.5 us
    pallas_call x1, Pallas kernels: 33.9 us -> 31.5 us  [shards(): pl.pallas_call(functools.partial(kernel, n), out_shape=jax.ShapeDtypeStru...]
where the time goes in v3:
time: 33.7 us; the launch traced here: 33.2 us
  Pallas kernels  31.5 us (93%)
  local copies, waits for them, and re-layouts  1.67 us (5%)
    pallas_call x1, Pallas kernels, shards(): pl.pallas_call(functools.partial(kernel, n), out_shape=jax.ShapeDtypeStru...  31.5 us
    unnamed x1, local copies, waits for them, and re-layouts  1.67 us

profile of v3, /device:TPU:2, one launch (start us, length us, event | category | flops | bytes accessed | tf_op | source)
XLA Modules:
  0.0 33.2 jit_solution(15607452801525579526)
XLA Ops:
  0.0 31.5 %shard_map.55 = f32[512,128]{1,0:T(8,128)} custom-call(bf16[8,2,4096]{2,1,0:T(2,128)(2,1)} %query_ref.1, bf16[512,2,4096]{2,1,0:T(2,128)(2,1)} %docs_ref.1, f32[2,64,64]{2,1,0:T(8,128)} %eig_ref.1, f32[2,64,64]{2,1,0:T(8,128)} %in_ref.1, f32[2,64,64]{2,1,0:T(8,128)} %out_basis_ref.1), custom_call_target="tpu_custom_call" | custom-call | flops 2147483648 | bytes 8388608 | tf_op jit(solution)/shard_map/pallas_call | solution.py:337
  31.6 1.7 %copy.7 = f32[512,128]{1,0:T(8,128)} copy(f32[512,128]{1,0:T(8,128)} %shard_map.55) | data formatting | bytes 524288
